TPU v7x, 128 devices: a whole 4x4x4 slice. The times are simulated.
128 devices in a mesh: row: 2 (over core), col: 2 (over x_hi), layer: 32 (over z, y, x_lo).
Axes of the slice: x: 4 (x_hi: 2, x_lo: 2; x = x_hi * 2 + x_lo), y: 4, z: 4, core: 2. Of those that a mesh axis runs over, the one named last changes fastest.
Arguments:
- flow: bfloat16 [4096, 16384], P('row', ('col', 'layer')), may hold values from 0.0099487305 to 1
- graph: bfloat16 [16384, 16384], P('col', 'layer'), may hold values from 6.0796738e-06 to 0.00024414062
- graph_pattern: int32 [128, 128], P('col', 'layer'), may hold values from 0 to 1, as said below
- out_pattern: int32 [32, 128], P(('row', 'col'), 'layer'), may hold values from 0 to 1, as said below
Outputs:
- new_flow: float32 [4096, 16384], P(('row', 'col'), 'layer')
Inputs may be any that keep to these rules, and one draw needn't show every extreme that they name: Every diagonal block graph_pattern[a, a] is 1; block rows differ in density. Every block column b has out_pattern[b % 32, b] = 1.
All inputs are finite; a program needn't handle non-finite values.
Results may differ from a plain program's by a relative error of at most 0.0003.
Values may be sent and summed in bfloat16 or wider, within the bound.
A program may use at most 256 MiB of HBM per device.

v0:
```python
import jax
import jax.numpy as jnp
from jax import lax
from jax.sharding import PartitionSpec as P

BLOCK = 128


def shards(flow, graph, graph_pattern, out_pattern):
    rows_here, cols_here = graph_pattern.shape
    blocked = graph.reshape(rows_here, BLOCK, cols_here, BLOCK)
    masked = (blocked * graph_pattern[:, None, :, None].astype(jnp.bfloat16)).reshape(graph.shape)
    left = lax.all_gather(flow, "layer", axis=1, tiled=True)
    expanded = lax.psum_scatter(
        jnp.dot(left, masked, preferred_element_type=jnp.float32),
        "col",
        scatter_dimension=0,
        tiled=True,
    )
    keep = out_pattern[:, None, :, None].astype(jnp.float32)
    slab_here = out_pattern.shape[0]
    inflated = ((expanded * expanded).reshape(slab_here, BLOCK, cols_here, BLOCK) * keep).reshape(
        expanded.shape
    )
    local_sums = jnp.sum(inflated, axis=0)
    totals = lax.psum(local_sums, ("row", "col"))
    all_rows = expanded.shape[0] * lax.axis_size("row") * lax.axis_size("col")
    return jnp.float32(all_rows) * inflated / totals[None, :]


def solution(mesh):
    placed = (
        P("row", ("col", "layer")),
        P("col", "layer"),
        P("col", "layer"),
        P(("row", "col"), "layer"),
    )
    return jax.shard_map(
        shards, mesh=mesh, in_specs=placed, out_specs=P(("row", "col"), "layer"), check_vma=False
    )
```

profile of v0, /device:TPU:1, one launch (start us, length us, event | category | flops | bytes accessed | tf_op | source)
XLA Modules:
  0.0 835.9 jit_solution(2841604644192751225)
XLA Ops:
  6.5 0.0 all-gather.2.cloned.1.call-start
  6.5 0.7 all-gather.2.cloned.1.call-update
  7.3 0.0 reduce-scatter.2.cloned.1.call-start
  7.3 0.7 convert_element_type.8
  8.0 0.1 copy.5
  8.1 711.7 %all-gather.2.cloned.1.call-done = bf16[2048,8192]{1,0:T(8,128)(2,1)} async-done(((bf16[2048,256]{1,0:T(8,128)(2,1)}), bf16[2048,8192]{1,0:T(8,128)(2,1)}) %all-gather.2.cloned.1.call-update) | async-done | bytes 33554448 | tf_op jit(solution)/shard_map/all_gather | solution.py:13
  719.8 5.4 mul.31
  725.2 27.4 %fusion.2 = f32[2048,512]{0,1:T(8,128)} fusion(bf16[2048,8192]{1,0:T(8,128)(2,1)} %all-gather.2.cloned.1.call-done, bf16[8192,512]{1,0:T(8,128)(2,1)} %param.5, bf16[1024,8,4,128]{3,2,1,0:T(4,128)(2,1)} %bitcast.22), kind=kOutput, calls=%fused_computation.3 | convolution fusion | flops 17184063488 | bytes 54525952 | tf_op jit(solution)/shard_map/dot_general | solution.py:15
  752.6 0.0 copy-start.1
  752.6 0.0 reduce-scatter.2.cloned.1.call-update
  752.6 0.7 copy-done.1
  753.3 58.8 %reduce-scatter.2.cloned.1.call-done = f32[1024,512]{0,1:T(8,128)} async-done(((f32[2048,512]{0,1:T(8,128)}), f32[1024,512]{0,1:T(8,128)}) %reduce-scatter.2.cloned.1.call-update) | async-done | bytes 2097168 | tf_op jit(solution)/shard_map/reduce_scatter | solution.py:14
  812.1 0.0 copy-start
  812.1 0.2 mul.35
  812.3 1.4 copy-done
  813.7 0.4 fusion.3
  814.1 8.3 psum.7
  822.5 3.7 multiply_divide_fusion
  826.2 2.9 copy.6
  (1 shorter events, 0.0 us)
Async XLA Ops:
  6.5 713.2 %all-gather.2.cloned.1.call-start = ((), (), s32[]{:S(2)}) async-start(), calls=%async_computation.1 | async-start | bytes 34603008 | tf_op jit(solution)/shard_map/all_gather | solution.py:13
  7.3 804.9 %reduce-scatter.2.cloned.1.call-start = ((), (), s32[]{:S(2)}) async-start(), calls=%async_computation.2 | async-start | bytes 6291456 | tf_op jit(solution)/shard_map/reduce_scatter | solution.py:14
  752.6 0.7 copy-start.1
  812.1 1.6 copy-start
Sparse Core Ops, SparseCore 0:
  8.9 710.7 all-gather.1
  752.8 59.2 reduce-scatter.1
where the time goes:
time: 836 us
  waiting for transfers between devices  771 us (92%)
  matrix products  27.4 us (3%)
  between operations  13.4 us (2%)
  local copies, waits for them, and re-layouts  10.7 us (1%)
    all_gather x1, waiting for transfers between devices, shards(): left = lax.all_gather(flow, 'layer', axis=1, tiled=True)  712 us
    reduce_scatter x1, waiting for transfers between devices, shards(): lax.psum_scatter(jnp.dot(left, masked, preferred_element_type=jnp.float32...  58.8 us
    dot_general x1, matrix products, shards(): jnp.dot(left, masked, preferred_element_type=jnp.float32)  27.4 us
  transfers between devices with their start and end apart: 2, of which 2 were waited for; matrix products, arithmetic and copies ran while one was open for 0% of the time, Pallas kernels for 0%

commit v1 on v0

v1 whole, which is shorter than its diff:
```python
import jax
import jax.numpy as jnp
from jax import lax
from jax.experimental import pallas as pl
from jax.experimental.pallas import tpu as pltpu
from jax.sharding import PartitionSpec as P

BLOCK = 128
SLABS = 8
Z = 4
Y = 4
MESH = pl.DeviceIdType.MESH


def kernel(
    flow_ref,
    graph_ref,
    gp_ref,
    op_ref,
    out_ref,
    tot_ref,
    a,
    b_own,
    b_par,
    b_out,
    own,
    c1s,
    c1r,
    c2s,
    c2r,
    c3s,
    c3r,
    sums,
    sums_in,
    g_send,
    g_recv,
    b_send,
    b_recv,
    f_send,
    f_recv,
    c_send,
    c_recv,
    o_sem,
    t_send,
    t_recv,
    l_sem,
):
    core = lax.axis_index("row")
    xh = lax.axis_index("col")
    layer = lax.axis_index("layer")
    z = layer // 8
    y = lax.rem(layer // 2, 4)
    xl = lax.rem(layer, 2)
    yn = (lax.rem(y + 1, 4), lax.rem(y + 3, 4))
    zn = (lax.rem(z + 1, 4), lax.rem(z + 3, 4))

    def at(zz, yy, xxl):
        return zz * 8 + yy * 2 + xxl

    y_dev = tuple((core, xh, at(z, v, xl)) for v in yn)
    z_dev = tuple((core, xh, at(v, y, xl)) for v in zn)
    pair = (core, xh, at(z, y, 1 - xl))
    cross = (core, 1 - xh, at(z, y, 1 - xl))
    sibling = (1 - core, xh, layer)
    opposite = (core, 1 - xh, layer)
    diagonal = (1 - core, 1 - xh, layer)
    peers = (sibling, opposite, diagonal)

    load_a = pltpu.make_async_copy(flow_ref, a.at[:, :, z, y], l_sem.at[0])
    load_a.start()
    load_bo = pltpu.make_async_copy(graph_ref.at[pl.ds(core * 8, 8), 1 - xl], b_out, l_sem.at[1])
    load_bo.start()
    load_b = pltpu.make_async_copy(graph_ref.at[:, xl], b_own, l_sem.at[2])
    load_b.start()

    barrier = pltpu.get_barrier_semaphore()
    for dev in (*y_dev, *z_dev, pair, cross, *peers):
        pl.semaphore_signal(barrier, inc=1, device_id=dev, device_id_type=MESH)
    pl.semaphore_wait(barrier, 9)

    def gather_copy(stage, f, d, s):
        first = y_dev if f == 0 else z_dev
        second = z_dev if f == 0 else y_dev
        back = 1 - d
        rows = pl.ds(64 * d, 64)
        if stage == 0:
            ref, dev = a.at[f, s, z, y], first[d]
        elif stage == 1:
            ref = a.at[f, s, z, yn[back], rows] if f == 0 else a.at[f, s, zn[back], y, rows]
            dev = first[d]
        elif stage == 2:
            ref = a.at[f, s, z] if f == 0 else a.at[f, s, :, y]
            dev = second[d]
        else:
            ref = a.at[f, s, zn[back], :, rows] if f == 0 else a.at[f, s, :, yn[back], rows]
            dev = second[d]
        return pltpu.make_async_remote_copy(
            src_ref=ref,
            dst_ref=ref,
            send_sem=g_send.at[stage, f, d, s],
            recv_sem=g_recv.at[stage, f, d, s],
            device_id=dev,
            device_id_type=MESH,
        )

    def remote(src, dst, send, recv, dev):
        return pltpu.make_async_remote_copy(
            src_ref=src, dst_ref=dst, send_sem=send, recv_sem=recv, device_id=dev, device_id_type=MESH
        )

    def issue(stage, s):
        for d in range(2):
            for f in range(2):
                if stage > 0:
                    if stage == 2 and d == 0:
                        gather_copy(1, f, 0, s).wait_recv()
                        gather_copy(1, f, 1, s).wait_recv()
                    elif stage != 2:
                        gather_copy(stage - 1, f, d, s).wait_recv()
                gather_copy(stage, f, d, s).start()

    def b_copy(j):
        return remote(b_out.at[j], b_par.at[core * 8 + j], b_send.at[j], b_recv.at[j], pair)

    def f_copy(j):
        ref = b_par.at[core * 8 + j]
        return remote(ref, ref, f_send.at[j], f_recv.at[j], sibling)

    def c_copy(k, s):
        src, dst, dev = ((c1s, c1r, cross), (c2s, c2r, pair), (c3s, c3r, cross))[k]
        return remote(src.at[s], dst.at[s], c_send.at[k, s], c_recv.at[k, s], dev)

    def out_copy(s):
        return pltpu.make_async_copy(own.at[s], out_ref.at[s], o_sem.at[s])

    def mask(ref, j, chunk, x):
        for r in range(2):
            for c in range(4):
                keep = gp_ref[(chunk * 2 + x) * 2 + r, c].astype(jnp.float32)
                rows, cols = pl.ds(r * BLOCK, BLOCK), pl.ds(c * BLOCK, BLOCK)
                ref[j, rows, cols] = (ref[j, rows, cols].astype(jnp.float32) * keep).astype(jnp.bfloat16)

    def rows_of(s):
        halves = []
        for h in (xh, 1 - xh):
            halves.append(jnp.concatenate([a[h, s, zz, yy] for zz in range(Z) for yy in range(Y)], axis=1))
        return jnp.concatenate(halves, axis=0)

    def product(s, b, n):
        cols = pl.ds(pl.multiple_of(n * 256, 256), 256)
        return jnp.dot(rows_of(s), b[:, :, cols].reshape(4096, 256), preferred_element_type=jnp.float32), cols

    def compute_own(s):
        @pl.loop(0, 2)
        def _(n):
            r, cols = product(s, b_own, n)
            own[s, :, cols] = r[:BLOCK]
            c1s[s, :, cols] = r[BLOCK:]

        c_copy(0, s).start()

    def compute_par(s):
        c_copy(0, s).wait_recv()

        @pl.loop(0, 2)
        def _(n):
            r, cols = product(s, b_par, n)
            c2s[s, :, cols] = r[:BLOCK] + c1r[s, :, cols]
            c3s[s, :, cols] = r[BLOCK:]

        c_copy(1, s).start()
        c_copy(2, s).start()

    def finish(s):
        c_copy(1, s).wait_recv()
        c_copy(2, s).wait_recv()
        for c in range(4):
            cols = pl.ds(c * BLOCK, BLOCK)
            keep = op_ref[s, c].astype(jnp.float32)
            v = own[s, :, cols] + c2r[s, :, cols] + c3r[s, :, cols]
            v = v * v * keep
            own[s, :, cols] = v
            sums[:, cols] += v.reshape(16, 8, BLOCK).sum(axis=0)
        out_copy(s).start()

    sums[...] = jnp.zeros_like(sums)
    load_a.wait()
    issue(0, 0)
    load_bo.wait()

    @pl.loop(0, 8)
    def _(j):
        mask(b_out, j, core * 8 + j, 1 - xl)
        b_copy(j).start()

    last = SLABS + 4

    def par_end(t):
        return jnp.clip(jnp.minimum(t - 3, 2 * (t - 6)), 0, SLABS)

    def fwd_end(t):
        return jnp.clip(2 * (t - 3) + 1, 0, 8)

    @pl.loop(1, last)
    def _(t):
        for stage in (3, 2, 1, 0):
            s = t - stage

            @pl.when((s >= 0) & (s < SLABS))
            def _():
                issue(stage, s)

        @pl.when(t == 3)
        def _():
            load_b.wait()

            @pl.loop(0, 16)
            def _(j):
                mask(b_own, j, j, xl)

        @pl.loop(fwd_end(t - 1), fwd_end(t))
        def _(j):
            b_copy(j).wait_recv()
            f_copy(j).start()

        @pl.when(t >= 4)
        def _():
            s = t - 4
            for f in range(2):
                for d in range(2):
                    gather_copy(3, f, d, s).wait_recv()
            compute_own(s)

        @pl.when(t == 7)
        def _():
            @pl.loop(0, 8)
            def _(j):
                f_copy(j).wait_recv()

        @pl.loop(par_end(t - 1), par_end(t))
        def _(s):
            compute_par(s)

        @pl.loop(par_end(t - 2), par_end(t - 1))
        def _(s):
            finish(s)

    @pl.loop(par_end(last - 2), par_end(last - 1))
    def _(s):
        finish(s)

    for k, dev in enumerate(peers):
        remote(sums, sums_in.at[k], t_send.at[k], t_recv.at[k], dev).start()

    @pl.loop(0, SLABS)
    def _(s):
        for stage in range(4):
            for f in range(2):
                for d in range(2):
                    gather_copy(stage, f, d, s).wait_send()
        for k in range(3):
            c_copy(k, s).wait_send()
        b_copy(s).wait_send()
        f_copy(s).wait_send()
        out_copy(s).wait()

    for k, dev in enumerate(peers):
        remote(sums, sums_in.at[k], t_send.at[k], t_recv.at[k], dev).wait()
    total = sums[...] + sums_in[0] + sums_in[1] + sums_in[2]
    tot_ref[...] = jnp.broadcast_to(total.sum(axis=0, keepdims=True), total.shape)


def shards(flow, graph, graph_pattern, out_pattern):
    f32, bf16 = jnp.float32, jnp.bfloat16
    dma = pltpu.SemaphoreType.DMA
    part = pltpu.VMEM((SLABS, BLOCK, 512), f32)
    inflated, totals = pl.pallas_call(
        kernel,
        out_shape=(
            jax.ShapeDtypeStruct((SLABS, BLOCK, 512), f32),
            jax.ShapeDtypeStruct((8, 512), f32),
        ),
        in_specs=[
            pl.BlockSpec(memory_space=pl.ANY),
            pl.BlockSpec(memory_space=pl.ANY),
            pl.BlockSpec(memory_space=pltpu.SMEM),
            pl.BlockSpec(memory_space=pltpu.SMEM),
        ],
        out_specs=(pl.BlockSpec(memory_space=pl.ANY), pl.BlockSpec(memory_space=pltpu.VMEM)),
        scratch_shapes=[
            pltpu.VMEM((2, SLABS, Z, Y, BLOCK, 256), bf16),
            pltpu.VMEM((16, 256, 512), bf16),
            pltpu.VMEM((16, 256, 512), bf16),
            pltpu.VMEM((8, 256, 512), bf16),
            part,
            part,
            part,
            part,
            part,
            part,
            part,
            pltpu.VMEM((8, 512), f32),
            pltpu.VMEM((3, 8, 512), f32),
            dma((4, 2, 2, SLABS)),
            dma((4, 2, 2, SLABS)),
            dma((8,)),
            dma((8,)),
            dma((8,)),
            dma((8,)),
            dma((3, SLABS)),
            dma((3, SLABS)),
            dma((SLABS,)),
            dma((3,)),
            dma((3,)),
            dma((3,)),
        ],
        compiler_params=pltpu.CompilerParams(
            collective_id=0, has_side_effects=True, vmem_limit_bytes=56 * 1024 * 1024
        ),
        cost_estimate=pl.CostEstimate(flops=2 * 2048 * 4096 * 1024, bytes_accessed=12 << 20, transcendentals=0),
    )(
        flow.reshape(2, SLABS, BLOCK, 256),
        graph.reshape(16, 2, 256, 512),
        graph_pattern,
        out_pattern,
    )
    return (jnp.float32(4096) * inflated / totals[0]).reshape(SLABS * BLOCK, 512)


def solution(mesh):
    placed = (
        P("row", ("col", "layer")),
        P("col", "layer"),
        P("col", "layer"),
        P(("row", "col"), "layer"),
    )
    return jax.shard_map(
        shards, mesh=mesh, in_specs=placed, out_specs=P(("row", "col"), "layer"), check_vma=False
    )
```

time: 836 us -> 162 us (0.19)
  waiting for transfers between devices: 771 us -> 0 us
  Pallas kernels: 0 us -> 155 us
  matrix products: 27.4 us -> 0 us
  between operations: 13.4 us -> 0.01 us
    all_gather x1 -> x0, waiting for transfers between devices: 712 us -> none  [shards(): left = lax.all_gather(flow, 'layer', axis=1, tiled=True)]
    pallas_call x0 -> x1, Pallas kernels: none -> 155 us  [shards(): pl.pallas_call(kernel, out_shape=(jax.ShapeDtypeStruct((SLABS, BLOCK, 512...]
    reduce_scatter x1 -> x0, waiting for transfers between devices: 58.8 us -> none  [shards(): lax.psum_scatter(jnp.dot(left, masked, preferred_element_type=jnp.float32...]
    dot_general x1 -> x0, matrix products: 27.4 us -> none  [shards(): jnp.dot(left, masked, preferred_element_type=jnp.float32)]
  transfers between devices with their start and end apart: 2 -> 0, of which waited for: 2 -> 0; matrix products, arithmetic and copies ran while one was open for 0% -> 0% of each run, Pallas kernels for 0% -> 0%
where the time goes in v1:
time: 162 us; the launch traced here: 161 us
  Pallas kernels  155 us (96%)
  local copies, waits for them, and re-layouts  3.45 us (2%)
  other arithmetic  3.35 us (2%)
    pallas_call x1, Pallas kernels, shards(): pl.pallas_call(kernel, out_shape=(jax.ShapeDtypeStruct((SLABS, BLOCK, 512...  155 us
    div x1, other arithmetic, shards(): jnp.float32(4096) * inflated / totals[0]  3.35 us

profile of v1, /device:TPU:1, one launch (start us, length us, event | category | flops | bytes accessed | tf_op | source)
XLA Modules:
  0.0 161.5 jit_solution(12766337474793185093)
XLA Ops:
  0.0 1.3 copy.6.op_ref
  1.3 1.4 copy.5.gp_ref
  2.7 154.7 %shard_map.46 = (f32[8,128,512]{2,1,0:T(8,128)}, f32[8,512]{1,0:T(8,128)}) custom-call(bf16[2,8,128,256]{3,2,1,0:T(8,128)(2,1)} %bitcast.6, bf16[16,2,256,512]{3,2,1,0:T(8,128)(2,1)} %bitcast.5, s32[64,4]{1,0:T(8,128)} %copy.5.gp_ref, s32[8,4]{1,0:T(8,128)} %copy.6.op_ref), custom_call_target="tpu_custom_call" | custom-call | flops 17179869184 | bytes 12582912 | tf_op jit(solution)/shard_map/pallas_call | solution.py:277
  157.4 0.7 slice.3
  158.1 3.3 %multiply_divide_fusion = f32[8,128,512]{2,1,0:T(8,128)} fusion(f32[8,128,512]{2,1,0:T(8,128)} %get-tuple-element.7, f32[512]{0:T(512)S(1)} %bitcast.4), kind=kLoop, calls=%fused_computation | loop fusion | flops 1048576 | bytes 4196352 | tf_op jit(solution)/shard_map/div | solution.py:327

commit v2 on v1

--- a/solution.py
+++ b/solution.py
@@ -6,7 +6,15 @@
 from jax.sharding import PartitionSpec as P
 
 BLOCK = 128
-SLABS = 8
+ROWS = 4096
+SLABS = 16
+HEIGHT = 1024 // SLABS
+HALF = HEIGHT // 2
+AHEAD = 3
+LAG = 2
+FORWARD_FROM = 7
+PARTNER_FROM = 15
+CODES = 65534.0
 Z = 4
 Y = 4
 MESH = pl.DeviceIdType.MESH
@@ -16,9 +24,8 @@
     flow_ref,
     graph_ref,
     gp_ref,
-    op_ref,
     out_ref,
-    tot_ref,
+    factor_ref,
     a,
     b_own,
     b_par,
@@ -30,6 +37,13 @@
     c2r,
     c3s,
     c3r,
+    m1s,
+    m1r,
+    m2s,
+    m2r,
+    m3s,
+    m3r,
+    gp,
     sums,
     sums_in,
     g_send,
@@ -40,6 +54,8 @@
     f_recv,
     c_send,
     c_recv,
+    m_send,
+    m_recv,
     o_sem,
     t_send,
     t_recv,
@@ -70,6 +86,8 @@
     load_a.start()
     load_bo = pltpu.make_async_copy(graph_ref.at[pl.ds(core * 8, 8), 1 - xl], b_out, l_sem.at[1])
     load_bo.start()
+    load_gp = pltpu.make_async_copy(gp_ref, gp, l_sem.at[3])
+    load_gp.start()
     load_b = pltpu.make_async_copy(graph_ref.at[:, xl], b_own, l_sem.at[2])
     load_b.start()
 
@@ -82,7 +100,7 @@
         first = y_dev if f == 0 else z_dev
         second = z_dev if f == 0 else y_dev
         back = 1 - d
-        rows = pl.ds(64 * d, 64)
+        rows = pl.ds(HALF * d, HALF)
         if stage == 0:
             ref, dev = a.at[f, s, z, y], first[d]
         elif stage == 1:
@@ -126,9 +144,24 @@
         ref = b_par.at[core * 8 + j]
         return remote(ref, ref, f_send.at[j], f_recv.at[j], sibling)
 
-    def c_copy(k, s):
-        src, dst, dev = ((c1s, c1r, cross), (c2s, c2r, pair), (c3s, c3r, cross))[k]
-        return remote(src.at[s], dst.at[s], c_send.at[k, s], c_recv.at[k, s], dev)
+    parts = ((c1s, c1r, m1s, m1r, cross), (c2s, c2r, m2s, m2r, pair), (c3s, c3r, m3s, m3r, cross))
+
+    def c_copies(k, s):
+        src, dst, top, top_in, dev = parts[k]
+        return (
+            remote(src.at[s], dst.at[s], c_send.at[k, s], c_recv.at[k, s], dev),
+            remote(top.at[s], top_in.at[s], m_send.at[k, s], m_recv.at[k, s], dev),
+        )
+
+    def encode(k, s, cols, v):
+        top = jnp.maximum(v.max(axis=0, keepdims=True), 1e-30)
+        code = (v * (CODES / top) + 0.5).astype(jnp.int32) - 32767
+        parts[k][0][s, :, cols] = code.astype(jnp.int16)
+        parts[k][2][s, :, cols] = top
+
+    def decode(k, s, cols):
+        code = parts[k][1][s, :, cols].astype(jnp.int32) + 32767
+        return code.astype(jnp.float32) * (parts[k][3][s, :, cols] * (1.0 / CODES))
 
     def out_copy(s):
         return pltpu.make_async_copy(own.at[s], out_ref.at[s], o_sem.at[s])
@@ -136,9 +169,11 @@
     def mask(ref, j, chunk, x):
         for r in range(2):
             for c in range(4):
-                keep = gp_ref[(chunk * 2 + x) * 2 + r, c].astype(jnp.float32)
+                keep = gp[(chunk * 2 + x) * 2 + r, c].astype(jnp.float32)
+                keep = jnp.full((16, BLOCK), keep, jnp.float32).astype(jnp.bfloat16)
                 rows, cols = pl.ds(r * BLOCK, BLOCK), pl.ds(c * BLOCK, BLOCK)
-                ref[j, rows, cols] = (ref[j, rows, cols].astype(jnp.float32) * keep).astype(jnp.bfloat16)
+                block = ref[j, rows, cols].reshape(8, 16, BLOCK) * keep
+                ref[j, rows, cols] = block.reshape(BLOCK, BLOCK)
 
     def rows_of(s):
         halves = []
@@ -154,67 +189,79 @@
         @pl.loop(0, 2)
         def _(n):
             r, cols = product(s, b_own, n)
-            own[s, :, cols] = r[:BLOCK]
-            c1s[s, :, cols] = r[BLOCK:]
-
-        c_copy(0, s).start()
+            own[s, :, cols] = r[:HEIGHT]
+            encode(0, s, cols, r[HEIGHT:])
+
+        for copy in c_copies(0, s):
+            copy.start()
 
     def compute_par(s):
-        c_copy(0, s).wait_recv()
+        for copy in c_copies(0, s):
+            copy.wait_recv()
 
         @pl.loop(0, 2)
         def _(n):
             r, cols = product(s, b_par, n)
-            c2s[s, :, cols] = r[:BLOCK] + c1r[s, :, cols]
-            c3s[s, :, cols] = r[BLOCK:]
-
-        c_copy(1, s).start()
-        c_copy(2, s).start()
+            encode(1, s, cols, r[:HEIGHT] + decode(0, s, cols))
+            encode(2, s, cols, r[HEIGHT:])
+
+        for k in (1, 2):
+            for copy in c_copies(k, s):
+                copy.start()
 
     def finish(s):
-        c_copy(1, s).wait_recv()
-        c_copy(2, s).wait_recv()
+        for k in (1, 2):
+            for copy in c_copies(k, s):
+                copy.wait_recv()
         for c in range(4):
             cols = pl.ds(c * BLOCK, BLOCK)
-            keep = op_ref[s, c].astype(jnp.float32)
-            v = own[s, :, cols] + c2r[s, :, cols] + c3r[s, :, cols]
+            keep = gp[64 + s * HEIGHT // BLOCK, c].astype(jnp.float32)
+            v = own[s, :, cols] + decode(1, s, cols) + decode(2, s, cols)
             v = v * v * keep
             own[s, :, cols] = v
-            sums[:, cols] += v.reshape(16, 8, BLOCK).sum(axis=0)
+            sums[:, cols] += v.reshape(HEIGHT // 8, 8, BLOCK).sum(axis=0)
         out_copy(s).start()
 
     sums[...] = jnp.zeros_like(sums)
     load_a.wait()
-    issue(0, 0)
+
+    @pl.loop(0, AHEAD + 1)
+    def _(s):
+        issue(0, s)
+
     load_bo.wait()
-
-    @pl.loop(0, 8)
-    def _(j):
+    load_gp.wait()
+    load_b.wait()
+
+    def send_b(j):
         mask(b_out, j, core * 8 + j, 1 - xl)
         b_copy(j).start()
 
-    last = SLABS + 4
+    send_b(0)
+    last = SLABS + 4 * LAG + 1
 
     def par_end(t):
-        return jnp.clip(jnp.minimum(t - 3, 2 * (t - 6)), 0, SLABS)
+        return jnp.clip(jnp.minimum(t - 4 * LAG, 3 * (t - PARTNER_FROM + 1)), 0, SLABS)
 
     def fwd_end(t):
-        return jnp.clip(2 * (t - 3) + 1, 0, 8)
+        return jnp.clip(t - FORWARD_FROM, 0, 8)
 
     @pl.loop(1, last)
     def _(t):
         for stage in (3, 2, 1, 0):
-            s = t - stage
+            s = t - LAG * stage + (AHEAD if stage == 0 else 0)
 
             @pl.when((s >= 0) & (s < SLABS))
             def _():
                 issue(stage, s)
 
-        @pl.when(t == 3)
+        @pl.when(t < 8)
         def _():
-            load_b.wait()
-
-            @pl.loop(0, 16)
+            send_b(t)
+
+        @pl.when(t < 5)
+        def _():
+            @pl.loop(4 * (t - 1), 4 * t)
             def _(j):
                 mask(b_own, j, j, xl)
 
@@ -223,15 +270,15 @@
             b_copy(j).wait_recv()
             f_copy(j).start()
 
-        @pl.when(t >= 4)
+        @pl.when((t >= 4 * LAG) & (t < SLABS + 4 * LAG))
         def _():
-            s = t - 4
+            s = t - 4 * LAG
             for f in range(2):
                 for d in range(2):
                     gather_copy(3, f, d, s).wait_recv()
             compute_own(s)
 
-        @pl.when(t == 7)
+        @pl.when(t == PARTNER_FROM)
         def _():
             @pl.loop(0, 8)
             def _(j):
@@ -241,11 +288,11 @@
         def _(s):
             compute_par(s)
 
-        @pl.loop(par_end(t - 2), par_end(t - 1))
+        @pl.loop(par_end(t - 3), par_end(t - 2))
         def _(s):
             finish(s)
 
-    @pl.loop(par_end(last - 2), par_end(last - 1))
+    @pl.loop(par_end(last - 3), par_end(last - 1))
     def _(s):
         finish(s)
 
@@ -259,46 +306,57 @@
                 for d in range(2):
                     gather_copy(stage, f, d, s).wait_send()
         for k in range(3):
-            c_copy(k, s).wait_send()
-        b_copy(s).wait_send()
-        f_copy(s).wait_send()
+            for copy in c_copies(k, s):
+                copy.wait_send()
         out_copy(s).wait()
+
+    @pl.loop(0, 8)
+    def _(j):
+        b_copy(j).wait_send()
+        f_copy(j).wait_send()
 
     for k, dev in enumerate(peers):
         remote(sums, sums_in.at[k], t_send.at[k], t_recv.at[k], dev).wait()
     total = sums[...] + sums_in[0] + sums_in[1] + sums_in[2]
-    tot_ref[...] = jnp.broadcast_to(total.sum(axis=0, keepdims=True), total.shape)
+    factor_ref[...] = jnp.float32(ROWS) / total.sum(axis=0, keepdims=True)
 
 
 def shards(flow, graph, graph_pattern, out_pattern):
     f32, bf16 = jnp.float32, jnp.bfloat16
     dma = pltpu.SemaphoreType.DMA
-    part = pltpu.VMEM((SLABS, BLOCK, 512), f32)
-    inflated, totals = pl.pallas_call(
+    part = pltpu.VMEM((SLABS, HEIGHT, 512), jnp.int16)
+    tops = pltpu.VMEM((SLABS, 1, 512), f32)
+    inflated, factor = pl.pallas_call(
         kernel,
         out_shape=(
-            jax.ShapeDtypeStruct((SLABS, BLOCK, 512), f32),
-            jax.ShapeDtypeStruct((8, 512), f32),
+            jax.ShapeDtypeStruct((SLABS, HEIGHT, 512), f32),
+            jax.ShapeDtypeStruct((1, 512), f32),
         ),
         in_specs=[
             pl.BlockSpec(memory_space=pl.ANY),
             pl.BlockSpec(memory_space=pl.ANY),
-            pl.BlockSpec(memory_space=pltpu.SMEM),
-            pl.BlockSpec(memory_space=pltpu.SMEM),
+            pl.BlockSpec(memory_space=pl.ANY),
         ],
         out_specs=(pl.BlockSpec(memory_space=pl.ANY), pl.BlockSpec(memory_space=pltpu.VMEM)),
         scratch_shapes=[
-            pltpu.VMEM((2, SLABS, Z, Y, BLOCK, 256), bf16),
+            pltpu.VMEM((2, SLABS, Z, Y, HEIGHT, 256), bf16),
             pltpu.VMEM((16, 256, 512), bf16),
             pltpu.VMEM((16, 256, 512), bf16),
             pltpu.VMEM((8, 256, 512), bf16),
-            part,
-            part,
-            part,
-            part,
-            part,
-            part,
-            part,
+            pltpu.VMEM((SLABS, HEIGHT, 512), f32),
+            part,
+            part,
+            part,
+            part,
+            part,
+            part,
+            tops,
+            tops,
+            tops,
+            tops,
+            tops,
+            tops,
+            pltpu.SMEM((72, 4), jnp.int32),
             pltpu.VMEM((8, 512), f32),
             pltpu.VMEM((3, 8, 512), f32),
             dma((4, 2, 2, SLABS)),
@@ -309,22 +367,23 @@
             dma((8,)),
             dma((3, SLABS)),
             dma((3, SLABS)),
+            dma((3, SLABS)),
+            dma((3, SLABS)),
             dma((SLABS,)),
             dma((3,)),
             dma((3,)),
-            dma((3,)),
+            dma((4,)),
         ],
         compiler_params=pltpu.CompilerParams(
             collective_id=0, has_side_effects=True, vmem_limit_bytes=56 * 1024 * 1024
         ),
         cost_estimate=pl.CostEstimate(flops=2 * 2048 * 4096 * 1024, bytes_accessed=12 << 20, transcendentals=0),
     )(
-        flow.reshape(2, SLABS, BLOCK, 256),
+        flow.reshape(2, SLABS, HEIGHT, 256),
         graph.reshape(16, 2, 256, 512),
-        graph_pattern,
-        out_pattern,
+        jnp.concatenate([graph_pattern, out_pattern]),
     )
-    return (jnp.float32(4096) * inflated / totals[0]).reshape(SLABS * BLOCK, 512)
+    return inflated.reshape(SLABS * HEIGHT, 512) * factor
 
 
 def solution(mesh):

time: 162 us -> 126 us (0.78)
  Pallas kernels: 155 us -> 121 us
  local copies, waits for them, and re-layouts: 3.45 us -> 0.71 us
    pallas_call x1, Pallas kernels: 155 us -> 121 us  [shards(): pl.pallas_call(kernel, out_shape=(jax.ShapeDtypeStruct((SLABS, HEIGHT, 51...]
    div x1 -> x0, other arithmetic: 3.35 us -> none  [shards(): jnp.float32(4096) * inflated / totals[0]]
    mul x0 -> x1, other arithmetic: none -> 3.16 us  [shards(): return inflated.reshape(SLABS * HEIGHT, 512) * factor]
    unnamed x2 -> x0, local copies, waits for them, and re-layouts: 2.73 us -> none
where the time goes in v2:
time: 126 us
  Pallas kernels  121 us (96%)
  other arithmetic  3.93 us (3%)
    pallas_call x1, Pallas kernels, shards(): pl.pallas_call(kernel, out_shape=(jax.ShapeDtypeStruct((SLABS, HEIGHT, 51...  121 us
    mul x1, other arithmetic, shards(): return inflated.reshape(SLABS * HEIGHT, 512) * factor  3.16 us

profile of v2, /device:TPU:1, one launch (start us, length us, event | category | flops | bytes accessed | tf_op | source)
XLA Modules:
  0.0 126.1 jit_solution(1440832285238254340)
XLA Ops:
  0.0 0.8 pad_add_fusion
  0.8 0.7 copy.7.gp_ref
  1.5 121.4 %shard_map.46 = (f32[16,64,512]{2,1,0:T(8,128)}, f32[1,512]{1,0:T(1,128)}) custom-call(bf16[2,16,64,256]{3,2,1,0:T(8,128)(2,1)} %bitcast.7, bf16[16,2,256,512]{3,2,1,0:T(8,128)(2,1)} %bitcast.6, s32[72,4]{1,0:T(8,128)} %copy.7.gp_ref), custom_call_target="tpu_custom_call" | custom-call | flops 17179869184 | bytes 12582912 | tf_op jit(solution)/shard_map/pallas_call | solution.py:329
  122.9 3.2 %bitcast_multiply_fusion = f32[1024,512]{1,0:T(8,128)} fusion(f32[16,64,512]{2,1,0:T(8,128)} %get-tuple-element.7, f32[512]{0:T(512)} %bitcast.5), kind=kLoop, calls=%fused_computation | loop fusion | flops 524288 | bytes 4196352 | tf_op jit(solution)/shard_map/mul | solution.py:386

commit v3 on v2

--- a/solution.py
+++ b/solution.py
@@ -12,8 +12,8 @@
 HALF = HEIGHT // 2
 AHEAD = 3
 LAG = 2
-FORWARD_FROM = 7
-PARTNER_FROM = 15
+FORWARD_FROM = 5
+PARTNER_FROM = 13
 CODES = 65534.0
 Z = 4
 Y = 4
@@ -24,6 +24,7 @@
     flow_ref,
     graph_ref,
     gp_ref,
+    op_ref,
     out_ref,
     factor_ref,
     a,
@@ -44,6 +45,7 @@
     m3s,
     m3r,
     gp,
+    op,
     sums,
     sums_in,
     g_send,
@@ -82,18 +84,21 @@
     diagonal = (1 - core, 1 - xh, layer)
     peers = (sibling, opposite, diagonal)
 
+    barrier = pltpu.get_barrier_semaphore()
+    for dev in (*y_dev, *z_dev, pair, cross, *peers):
+        pl.semaphore_signal(barrier, inc=1, device_id=dev, device_id_type=MESH)
+
     load_a = pltpu.make_async_copy(flow_ref, a.at[:, :, z, y], l_sem.at[0])
     load_a.start()
     load_bo = pltpu.make_async_copy(graph_ref.at[pl.ds(core * 8, 8), 1 - xl], b_out, l_sem.at[1])
     load_bo.start()
     load_gp = pltpu.make_async_copy(gp_ref, gp, l_sem.at[3])
     load_gp.start()
+    load_op = pltpu.make_async_copy(op_ref, op, l_sem.at[4])
+    load_op.start()
     load_b = pltpu.make_async_copy(graph_ref.at[:, xl], b_own, l_sem.at[2])
     load_b.start()
 
-    barrier = pltpu.get_barrier_semaphore()
-    for dev in (*y_dev, *z_dev, pair, cross, *peers):
-        pl.semaphore_signal(barrier, inc=1, device_id=dev, device_id_type=MESH)
     pl.semaphore_wait(barrier, 9)
 
     def gather_copy(stage, f, d, s):
@@ -102,7 +107,7 @@
         back = 1 - d
         rows = pl.ds(HALF * d, HALF)
         if stage == 0:
-            ref, dev = a.at[f, s, z, y], first[d]
+            ref, src, dev = a.at[f, s, z, y], flow_ref.at[f, s], first[d]
         elif stage == 1:
             ref = a.at[f, s, z, yn[back], rows] if f == 0 else a.at[f, s, zn[back], y, rows]
             dev = first[d]
@@ -113,7 +118,7 @@
             ref = a.at[f, s, zn[back], :, rows] if f == 0 else a.at[f, s, :, yn[back], rows]
             dev = second[d]
         return pltpu.make_async_remote_copy(
-            src_ref=ref,
+            src_ref=src if stage == 0 else ref,
             dst_ref=ref,
             send_sem=g_send.at[stage, f, d, s],
             recv_sem=g_recv.at[stage, f, d, s],
@@ -137,6 +142,12 @@
                         gather_copy(stage - 1, f, d, s).wait_recv()
                 gather_copy(stage, f, d, s).start()
 
+    def drain(s):
+        for stage in range(4):
+            for f in range(2):
+                for d in range(2):
+                    gather_copy(stage, f, d, s).wait_send()
+
     def b_copy(j):
         return remote(b_out.at[j], b_par.at[core * 8 + j], b_send.at[j], b_recv.at[j], pair)
 
@@ -146,8 +157,10 @@
 
     parts = ((c1s, c1r, m1s, m1r, cross), (c2s, c2r, m2s, m2r, pair), (c3s, c3r, m3s, m3r, cross))
 
-    def c_copies(k, s):
+    def c_copies(k, s, direct=False):
         src, dst, top, top_in, dev = parts[k]
+        if direct:
+            dev = opposite
         return (
             remote(src.at[s], dst.at[s], c_send.at[k, s], c_recv.at[k, s], dev),
             remote(top.at[s], top_in.at[s], m_send.at[k, s], m_recv.at[k, s], dev),
@@ -169,7 +182,7 @@
     def mask(ref, j, chunk, x):
         for r in range(2):
             for c in range(4):
-                keep = gp[(chunk * 2 + x) * 2 + r, c].astype(jnp.float32)
+                keep = gp[c, (chunk * 2 + x) * 2 + r].astype(jnp.float32)
                 keep = jnp.full((16, BLOCK), keep, jnp.float32).astype(jnp.bfloat16)
                 rows, cols = pl.ds(r * BLOCK, BLOCK), pl.ds(c * BLOCK, BLOCK)
                 block = ref[j, rows, cols].reshape(8, 16, BLOCK) * keep
@@ -185,52 +198,58 @@
         cols = pl.ds(pl.multiple_of(n * 256, 256), 256)
         return jnp.dot(rows_of(s), b[:, :, cols].reshape(4096, 256), preferred_element_type=jnp.float32), cols
 
-    def compute_own(s):
+    def compute_own(s, direct=False):
         @pl.loop(0, 2)
         def _(n):
             r, cols = product(s, b_own, n)
             own[s, :, cols] = r[:HEIGHT]
             encode(0, s, cols, r[HEIGHT:])
 
-        for copy in c_copies(0, s):
+        for copy in c_copies(0, s, direct):
             copy.start()
 
-    def compute_par(s):
-        for copy in c_copies(0, s):
-            copy.wait_recv()
+    def compute_par(s, direct=False):
+        if not direct:
+            for copy in c_copies(0, s):
+                copy.wait_recv()
 
         @pl.loop(0, 2)
         def _(n):
             r, cols = product(s, b_par, n)
-            encode(1, s, cols, r[:HEIGHT] + decode(0, s, cols))
+            encode(1, s, cols, r[:HEIGHT] if direct else r[:HEIGHT] + decode(0, s, cols))
             encode(2, s, cols, r[HEIGHT:])
 
         for k in (1, 2):
             for copy in c_copies(k, s):
                 copy.start()
 
-    def finish(s):
-        for k in (1, 2):
-            for copy in c_copies(k, s):
+    def finish(s, direct=False):
+        came = (1, 2, 0) if direct else (1, 2)
+        for k in came:
+            for copy in c_copies(k, s, direct and k == 0):
                 copy.wait_recv()
         for c in range(4):
             cols = pl.ds(c * BLOCK, BLOCK)
-            keep = gp[64 + s * HEIGHT // BLOCK, c].astype(jnp.float32)
-            v = own[s, :, cols] + decode(1, s, cols) + decode(2, s, cols)
+            keep = op[c, s * HEIGHT // BLOCK].astype(jnp.float32)
+            v = own[s, :, cols] + sum(decode(k, s, cols) for k in came)
             v = v * v * keep
             own[s, :, cols] = v
             sums[:, cols] += v.reshape(HEIGHT // 8, 8, BLOCK).sum(axis=0)
         out_copy(s).start()
+        for k in range(3):
+            for copy in c_copies(k, s, direct and k == 0):
+                copy.wait_send()
 
     sums[...] = jnp.zeros_like(sums)
-    load_a.wait()
 
     @pl.loop(0, AHEAD + 1)
     def _(s):
         issue(0, s)
 
     load_bo.wait()
+    load_a.wait()
     load_gp.wait()
+    load_op.wait()
     load_b.wait()
 
     def send_b(j):
@@ -238,10 +257,10 @@
         b_copy(j).start()
 
     send_b(0)
-    last = SLABS + 4 * LAG + 1
+    last = SLABS + 4 * LAG
 
     def par_end(t):
-        return jnp.clip(jnp.minimum(t - 4 * LAG, 3 * (t - PARTNER_FROM + 1)), 0, SLABS)
+        return jnp.clip(jnp.minimum(t - 4 * LAG, 4 * (t - PARTNER_FROM + 1)), 0, SLABS)
 
     def fwd_end(t):
         return jnp.clip(t - FORWARD_FROM, 0, 8)
@@ -270,7 +289,7 @@
             b_copy(j).wait_recv()
             f_copy(j).start()
 
-        @pl.when((t >= 4 * LAG) & (t < SLABS + 4 * LAG))
+        @pl.when((t >= 4 * LAG) & (t < last - 1))
         def _():
             s = t - 4 * LAG
             for f in range(2):
@@ -292,28 +311,37 @@
         def _(s):
             finish(s)
 
-    @pl.loop(par_end(last - 3), par_end(last - 1))
+        @pl.when(t > 4 * LAG)
+        def _():
+            drain(t - 4 * LAG - 1)
+
+        @pl.when(t == PARTNER_FROM + 1)
+        def _():
+            @pl.loop(0, 8)
+            def _(j):
+                b_copy(j).wait_send()
+                f_copy(j).wait_send()
+
+    for f in range(2):
+        for d in range(2):
+            gather_copy(3, f, d, SLABS - 1).wait_recv()
+    compute_own(SLABS - 1, True)
+    compute_par(SLABS - 1, True)
+
+    @pl.loop(par_end(last - 3), SLABS - 1)
     def _(s):
         finish(s)
 
+    finish(SLABS - 1, True)
+
     for k, dev in enumerate(peers):
         remote(sums, sums_in.at[k], t_send.at[k], t_recv.at[k], dev).start()
 
+    drain(SLABS - 1)
+
     @pl.loop(0, SLABS)
     def _(s):
-        for stage in range(4):
-            for f in range(2):
-                for d in range(2):
-                    gather_copy(stage, f, d, s).wait_send()
-        for k in range(3):
-            for copy in c_copies(k, s):
-                copy.wait_send()
         out_copy(s).wait()
-
-    @pl.loop(0, 8)
-    def _(j):
-        b_copy(j).wait_send()
-        f_copy(j).wait_send()
 
     for k, dev in enumerate(peers):
         remote(sums, sums_in.at[k], t_send.at[k], t_recv.at[k], dev).wait()
@@ -336,6 +364,7 @@
             pl.BlockSpec(memory_space=pl.ANY),
             pl.BlockSpec(memory_space=pl.ANY),
             pl.BlockSpec(memory_space=pl.ANY),
+            pl.BlockSpec(memory_space=pl.ANY),
         ],
         out_specs=(pl.BlockSpec(memory_space=pl.ANY), pl.BlockSpec(memory_space=pltpu.VMEM)),
         scratch_shapes=[
@@ -356,7 +385,8 @@
             tops,
             tops,
             tops,
-            pltpu.SMEM((72, 4), jnp.int32),
+            pltpu.SMEM((4, 64), jnp.int32),
+            pltpu.SMEM((4, 8), jnp.int32),
             pltpu.VMEM((8, 512), f32),
             pltpu.VMEM((3, 8, 512), f32),
             dma((4, 2, 2, SLABS)),
@@ -372,7 +402,7 @@
             dma((SLABS,)),
             dma((3,)),
             dma((3,)),
-            dma((4,)),
+            dma((5,)),
         ],
         compiler_params=pltpu.CompilerParams(
             collective_id=0, has_side_effects=True, vmem_limit_bytes=56 * 1024 * 1024
@@ -381,7 +411,8 @@
     )(
         flow.reshape(2, SLABS, HEIGHT, 256),
         graph.reshape(16, 2, 256, 512),
-        jnp.concatenate([graph_pattern, out_pattern]),
+        graph_pattern.T,
+        out_pattern.T,
     )
     return inflated.reshape(SLABS * HEIGHT, 512) * factor
 

time: 126 us -> 122 us (0.968)
  Pallas kernels: 121 us -> 119 us
    pallas_call x1, Pallas kernels: 121 us -> 119 us  [shards(): pl.pallas_call(kernel, out_shape=(jax.ShapeDtypeStruct((SLABS, HEIGHT, 51...]
where the time goes in v3:
time: 122 us
  Pallas kernels  119 us (98%)
  other arithmetic  3.16 us (3%)
    pallas_call x1, Pallas kernels, shards(): pl.pallas_call(kernel, out_shape=(jax.ShapeDtypeStruct((SLABS, HEIGHT, 51...  119 us
    mul x1, other arithmetic, shards(): return inflated.reshape(SLABS * HEIGHT, 512) * factor  3.16 us

profile of v3, /device:TPU:1, one launch (start us, length us, event | category | flops | bytes accessed | tf_op | source)
XLA Modules:
  0.0 121.7 jit_solution(11411188381748625878)
XLA Ops:
  0.0 118.6 %shard_map.46 = (f32[16,64,512]{2,1,0:T(8,128)}, f32[1,512]{1,0:T(1,128)}) custom-call(bf16[2,16,64,256]{3,2,1,0:T(8,128)(2,1)} %bitcast.9, bf16[16,2,256,512]{3,2,1,0:T(8,128)(2,1)} %bitcast.8, s32[4,64]{1,0:T(4,128)} %bitcast.10, s32[4,8]{1,0:T(4,128)} %bitcast.11), custom_call_target="tpu_custom_call" | custom-call | flops 17179869184 | bytes 12582912 | tf_op jit(solution)/shard_map/pallas_call | solution.py:357
  118.6 3.2 %bitcast_multiply_fusion = f32[1024,512]{1,0:T(8,128)} fusion(f32[16,64,512]{2,1,0:T(8,128)} %get-tuple-element.7, f32[512]{0:T(512)} %bitcast.7), kind=kLoop, calls=%fused_computation | loop fusion | flops 524288 | bytes 4196352 | tf_op jit(solution)/shard_map/mul | solution.py:417

commit v4 on v3

--- a/solution.py
+++ b/solution.py
@@ -242,21 +242,21 @@
 
     sums[...] = jnp.zeros_like(sums)
 
-    @pl.loop(0, AHEAD + 1)
-    def _(s):
-        issue(0, s)
-
+    issue(0, 0)
     load_bo.wait()
-    load_a.wait()
     load_gp.wait()
     load_op.wait()
-    load_b.wait()
 
     def send_b(j):
         mask(b_out, j, core * 8 + j, 1 - xl)
         b_copy(j).start()
 
     send_b(0)
+
+    @pl.loop(1, AHEAD + 1)
+    def _(s):
+        issue(0, s)
+
     last = SLABS + 4 * LAG
 
     def par_end(t):
@@ -267,7 +267,7 @@
 
     @pl.loop(1, last)
     def _(t):
-        for stage in (3, 2, 1, 0):
+        for stage in (2, 3, 1, 0):
             s = t - LAG * stage + (AHEAD if stage == 0 else 0)
 
             @pl.when((s >= 0) & (s < SLABS))
@@ -278,9 +278,17 @@
         def _():
             send_b(t)
 
-        @pl.when(t < 5)
-        def _():
-            @pl.loop(4 * (t - 1), 4 * t)
+        @pl.when(t == 2)
+        def _():
+            load_a.wait()
+
+        @pl.when(t == 4)
+        def _():
+            load_b.wait()
+
+        @pl.when((t >= 4) & (t < 8))
+        def _():
+            @pl.loop(4 * (t - 4), 4 * (t - 3))
             def _(j):
                 mask(b_own, j, j, xl)
 

time: 122 us -> 122 us (level)
  no operation moved by 1% of the time
where the time goes in v4:
time: 122 us
  Pallas kernels  119 us (98%)
  other arithmetic  3.16 us (3%)
    pallas_call x1, Pallas kernels, shards(): pl.pallas_call(kernel, out_shape=(jax.ShapeDtypeStruct((SLABS, HEIGHT, 51...  119 us
    mul x1, other arithmetic, shards(): return inflated.reshape(SLABS * HEIGHT, 512) * factor  3.16 us

profile of v4, /device:TPU:1, one launch (start us, length us, event | category | flops | bytes accessed | tf_op | source)
XLA Modules:
  0.0 121.8 jit_solution(16681687707386736698)
XLA Ops:
  0.0 118.6 %shard_map.46 = (f32[16,64,512]{2,1,0:T(8,128)}, f32[1,512]{1,0:T(1,128)}) custom-call(bf16[2,16,64,256]{3,2,1,0:T(8,128)(2,1)} %bitcast.9, bf16[16,2,256,512]{3,2,1,0:T(8,128)(2,1)} %bitcast.8, s32[4,64]{1,0:T(4,128)} %bitcast.10, s32[4,8]{1,0:T(4,128)} %bitcast.11), custom_call_target="tpu_custom_call" | custom-call | flops 17179869184 | bytes 12582912 | tf_op jit(solution)/shard_map/pallas_call | solution.py:365
  118.6 3.2 %bitcast_multiply_fusion = f32[1024,512]{1,0:T(8,128)} fusion(f32[16,64,512]{2,1,0:T(8,128)} %get-tuple-element.7, f32[512]{0:T(512)} %bitcast.7), kind=kLoop, calls=%fused_computation | loop fusion | flops 524288 | bytes 4196352 | tf_op jit(solution)/shard_map/mul | solution.py:425
